TPU v7x, 256 devices: a whole 4x4x8 slice. The times are simulated.
256 devices in a mesh: paper: 32 (over x_lo, z, core), type: 8 (over y, x_hi).
Axes of the slice: x: 4 (x_hi: 2, x_lo: 2; x = x_hi * 2 + x_lo), y: 4, z: 8, core: 2. Of those that a mesh axis runs over, the one named last changes fastest.
Arguments:
- papers: bfloat16 [131072, 512], P(('paper', 'type')), may hold values from -6 to 6
- cited_rows: bfloat16 [4096, 512], P('paper'), may hold values from -6 to 6
- entities: bfloat16 [1024, 512], P('type'), may hold values from -6 to 6
- entity_kinds: int32 [1024], P('type'), may hold values from 0 to 1
- query_weight: bfloat16 [512, 512], replicated, may hold values from -0.25 to 0.25
- key_weight: bfloat16 [3, 512, 512], replicated, may hold values from -0.25 to 0.25
- value_weight: bfloat16 [3, 512, 512], replicated, may hold values from -0.25 to 0.25
- attention_rel: bfloat16 [4, 8, 64, 64], replicated, may hold values from -0.75 to 0.75
- message_rel: bfloat16 [4, 8, 64, 64], replicated, may hold values from -0.75 to 0.75
- relation_prior: float32 [4, 8], replicated, may hold values from 0.5 to 2.5
- output_weight: bfloat16 [512, 512], replicated, may hold values from -0.25 to 0.25
- skip_gate: float32 [1], replicated, may hold values from -1 to 1
- norm_gain: float32 [512], replicated, may hold values from 0.5 to 1.5
- cite_pattern: int32 [1024, 8, 128, 128], P(('paper', 'type')), may hold values from 0 to 1, as said below
- cite_tiles: int32 [1024, 8], P(('paper', 'type')), may hold values from 0 to 31, as said below
- cite_counts: int32 [1024, 8], P(('paper', 'type')), may hold values from 0 to 16384, as said below
- entity_pattern: int32 [1024, 2, 128, 128], P(('paper', 'type')), may hold values from 0 to 1, as said below
- entity_tiles: int32 [1024, 2], P(('paper', 'type')), may hold values from 0 to 7, as said below
- entity_counts: int32 [1024, 2], P(('paper', 'type')), may hold values from 0 to 16384, as said below
Outputs:
- updated: bfloat16 [131072, 512], P(('paper', 'type'))
Inputs may be any that keep to these rules, and one draw needn't show every extreme that they name: `cite_pattern`: entry [a, k, p, c] is 1 where paper 128 * a + p has an edge from source 128 * cite_tiles[a, k] + c, else 0. A tile of papers uses its first 8, 4, 2 or 1 slots (at least one), the same number for all tiles of one device's papers; later slots are all zero. `cite_tiles`: the slots of one tile name distinct tiles. `cite_counts`: the number of ones in the slot's block. `entity_pattern`: as cite_pattern, with sources 128 * entity_tiles[a, k] + c; a tile uses its first 1 to 2 slots, later slots are all zero. `entity_tiles`: the slots of one tile name distinct tiles. `entity_counts`: the number of ones in the slot's block.
All inputs are finite; a program needn't handle non-finite values.
Results may differ from a plain program's by a relative error of at most 0.0087.
Values may be sent and summed in bfloat16 or wider, within the bound.
No kernel may reach another device: no remote copies, remote signals or barrier semaphores. Data moves between devices by JAX's collectives and lax.ppermute only.
A program may use at most 128 MiB of HBM per device.

v0:
```python
import math
import jax
import jax.numpy as jnp
from jax import lax
from jax.sharding import PartitionSpec as P

CAP = 20.0


def head_split(matrix, head_count):
    return matrix.reshape(matrix.shape[0], head_count, matrix.shape[1] // head_count)


def relate(raw_rows, weight):
    head_count = weight.shape[0]
    mapped = jnp.einsum(
        "nhd,hde->nhe", head_split(raw_rows, head_count), weight, preferred_element_type=jnp.float32
    )
    return mapped.reshape(raw_rows.shape)


def project(source_rows, weight):
    return jnp.dot(source_rows, weight, preferred_element_type=jnp.float32).astype(jnp.bfloat16)


def cited_pairs(source_rows, key_weight, value_weight, attention_rel, message_rel):
    key_rows = relate(project(source_rows, key_weight[0]), attention_rel[0]).astype(jnp.bfloat16)
    value_rows = relate(project(source_rows, value_weight[0]), message_rel[0]).astype(jnp.bfloat16)
    return (key_rows, value_rows)


def entity_side(source_rows, kind_ids, key_weight, value_weight, attention_rel, message_rel):
    author = (kind_ids == 0)[:, None]
    key_raw = jnp.where(
        author,
        jnp.dot(source_rows, key_weight[1], preferred_element_type=jnp.float32),
        jnp.dot(source_rows, key_weight[2], preferred_element_type=jnp.float32),
    ).astype(jnp.bfloat16)
    value_raw = jnp.where(
        author,
        jnp.dot(source_rows, value_weight[1], preferred_element_type=jnp.float32),
        jnp.dot(source_rows, value_weight[2], preferred_element_type=jnp.float32),
    ).astype(jnp.bfloat16)
    key_rows = jnp.where(
        author, relate(key_raw, attention_rel[1]), relate(key_raw, attention_rel[2])
    ).astype(jnp.bfloat16)
    value_rows = jnp.where(
        author, relate(value_raw, message_rel[1]), relate(value_raw, message_rel[2])
    ).astype(jnp.bfloat16)
    return (key_rows, value_rows)


def kind_scales(kind_ids, relation_prior, inv_root):
    author = (kind_ids == 0)[:, None]
    return jnp.where(author, relation_prior[1][None, :], relation_prior[2][None, :]) * inv_root


def own_term(query_heads, own_key, own_value, scale):
    head_count = query_heads.shape[1]
    own_dot = jnp.sum(
        query_heads.astype(jnp.float32) * head_split(own_key, head_count).astype(jnp.float32),
        axis=2,
    )
    weights = jnp.exp(CAP * jnp.tanh(own_dot * scale / CAP))
    rounded = lax.optimization_barrier(weights.astype(jnp.bfloat16)).astype(jnp.float32)
    return (rounded[:, :, None] * head_split(own_value, head_count).astype(jnp.float32), weights)


def dense_live(pattern, tile_ids, counts, source_count):
    chosen = (tile_ids[:, :, None] == jnp.arange(source_count, dtype=jnp.int32)[None, None, :]) & (
        counts[:, :, None] > 0
    )
    spread = jnp.einsum(
        "ikj,ikac->iajc",
        chosen.astype(jnp.bfloat16),
        pattern.astype(jnp.bfloat16),
        preferred_element_type=jnp.float32,
    )
    return (
        spread.reshape(pattern.shape[0] * pattern.shape[2], source_count * pattern.shape[3]) > 0.5
    )


def attend(running, query_heads, key_rows, value_rows, scales, live_mask):
    head_count = query_heads.shape[1]
    products = jnp.einsum(
        "thd,shd->hts",
        query_heads,
        head_split(key_rows, head_count),
        preferred_element_type=jnp.float32,
    )
    scores = products * scales.T[:, None, :]
    scores = CAP * jnp.tanh(scores / CAP)
    weights = jnp.where(live_mask[None, :, :], jnp.exp(scores), 0.0)
    numerator, denominator = running
    numerator = numerator + jnp.einsum(
        "hts,shd->thd",
        weights.astype(jnp.bfloat16),
        head_split(value_rows, head_count),
        preferred_element_type=jnp.float32,
    )
    denominator = denominator + jnp.sum(weights, axis=2).T
    return (numerator, denominator)


def sweep_dense(running, query_heads, key_rows, value_rows, scales, live_mask):
    row_count = key_rows.shape[0]
    block_rows = math.gcd(row_count, 512)
    block_count = row_count // block_rows

    def single_block(offset, state):
        part_keys = lax.dynamic_slice_in_dim(key_rows, offset, block_rows, 0)
        part_values = lax.dynamic_slice_in_dim(value_rows, offset, block_rows, 0)
        part_scales = lax.dynamic_slice_in_dim(scales, offset, block_rows, 0)
        part_live = lax.dynamic_slice_in_dim(live_mask, offset, block_rows, 1)
        return attend(state, query_heads, part_keys, part_values, part_scales, part_live)

    return lax.fori_loop(
        0, block_count, lambda position, state: single_block(position * block_rows, state), running
    )


def per_device(
    papers,
    cited_rows,
    entities,
    entity_kinds,
    query_weight,
    key_weight,
    value_weight,
    attention_rel,
    message_rel,
    relation_prior,
    output_weight,
    skip_gate,
    norm_gain,
    cite_pattern,
    cite_tiles,
    cite_counts,
    entity_pattern,
    entity_tiles,
    entity_counts,
):
    head_count = relation_prior.shape[1]
    model_width = papers.shape[1]
    inv_root = 1.0 / math.sqrt(model_width // head_count)
    tile_size = cite_pattern.shape[2]
    query_heads = head_split(project(papers, query_weight), head_count)
    own_keys = relate(project(papers, key_weight[0]), attention_rel[3]).astype(jnp.bfloat16)
    own_values = relate(project(papers, value_weight[0]), message_rel[3]).astype(jnp.bfloat16)
    running = own_term(query_heads, own_keys, own_values, relation_prior[3] * inv_root)
    cite_sources = cited_rows.shape[0] * lax.axis_size("paper") // tile_size
    entity_sources = entities.shape[0] * lax.axis_size("type") // tile_size
    cite_live = dense_live(cite_pattern, cite_tiles, cite_counts, cite_sources)
    entity_live = dense_live(entity_pattern, entity_tiles, entity_counts, entity_sources)
    cite_scale = relation_prior[0] * inv_root

    def sweep_rows(state, key_rows, value_rows, scales, live_mask):
        return sweep_dense(state, query_heads, key_rows, value_rows, scales, live_mask)

    cite_keys, cite_values = cited_pairs(
        cited_rows, key_weight, value_weight, attention_rel, message_rel
    )
    key_rows = lax.all_gather(cite_keys, "paper", axis=0, tiled=True)
    value_rows = lax.all_gather(cite_values, "paper", axis=0, tiled=True)
    row_count = key_rows.shape[0]
    scales = jnp.broadcast_to(cite_scale[None, :], (row_count, head_count))
    live_mask = cite_live
    running = sweep_rows(running, key_rows, value_rows, scales, live_mask)
    entity_keys, entity_values = entity_side(
        entities, entity_kinds, key_weight, value_weight, attention_rel, message_rel
    )
    key_rows = lax.all_gather(entity_keys, "type", axis=0, tiled=True)
    value_rows = lax.all_gather(entity_values, "type", axis=0, tiled=True)
    kind_ids = lax.all_gather(entity_kinds, "type", axis=0, tiled=True)
    live_mask = entity_live
    scales = kind_scales(kind_ids, relation_prior, inv_root)
    running = sweep_rows(running, key_rows, value_rows, scales, live_mask)
    numerator, denominator = running
    mixed = numerator / denominator[:, :, None]
    hidden = jax.nn.gelu(mixed, approximate=False).reshape(papers.shape).astype(jnp.bfloat16)
    projected = jnp.dot(hidden, output_weight, preferred_element_type=jnp.float32)
    alpha = jax.nn.sigmoid(skip_gate[0])
    blended = alpha * projected + (1.0 - alpha) * papers.astype(jnp.float32)
    centre = jnp.mean(blended, axis=1, keepdims=True)
    spread = jnp.mean(jnp.square(blended - centre), axis=1, keepdims=True)
    return ((blended - centre) * lax.rsqrt(spread + 1e-05) * norm_gain).astype(jnp.bfloat16)


def solution(mesh):
    in_specs = (
        P(("paper", "type"), None),
        P("paper", None),
        P("type", None),
        P("type"),
        P(),
        P(),
        P(),
        P(),
        P(),
        P(),
        P(),
        P(),
        P(),
        P(("paper", "type"), None, None, None),
        P(("paper", "type"), None),
        P(("paper", "type"), None),
        P(("paper", "type"), None, None, None),
        P(("paper", "type"), None),
        P(("paper", "type"), None),
    )
    out_specs = P(("paper", "type"), None)
    return jax.shard_map(
        per_device, mesh=mesh, in_specs=in_specs, out_specs=out_specs, check_vma=False
    )
```

profile of v0, /device:TPU:32, one launch (start us, length us, event | category | flops | bytes accessed | tf_op | source)
XLA Modules:
  0.0 305.5 jit_solution(12606027069432902656)
XLA Ops:
  6.5 1.4 convolution_convert_fusion.6
  8.1 1.8 convolution_convert_fusion.8
  10.0 1.5 convolution_convert_fusion.5
  11.6 1.8 convolution_convert_fusion.7
  14.1 1.3 fusion.50
  15.4 1.4 fusion.37
  18.8 1.3 fusion.53
  20.2 1.4 fusion.36
  26.8 1.8 select_convert_fusion
  29.2 2.3 convolution_convert_fusion.3
  31.5 2.4 convolution_convert_fusion.2
  34.9 1.5 convolution_convert_fusion.4
  36.5 1.6 fusion.35
  39.2 2.5 broadcast_compare_fusion
  41.7 3.0 copy.131
  44.7 23.5 %all-gather = s32[8,1,128]{2,1,0:T(1,128)S(1)} all-gather(s32[1,1,128]{2,1,0:T(1,128)S(1)} %bitcast.259), channel_id=1, replica_groups=mesh['paper'=32,'type'=8] {'type'}, dimensions={0}, use_global_device_ids=true | all-gather | bytes 4608 | tf_op jit(solution)/shard_map/all_gather | solution.py:175
  70.2 2.3 fusion.34
  72.5 12.5 %all-gather.6.cloned.1.call-done = bf16[4096,512]{0,1:T(8,128)(2,1)} async-done(((bf16[128,512]{0,1:T(8,128)(2,1)}), bf16[4096,512]{0,1:T(8,128)(2,1)}) %all-gather.6.cloned.1.call-update) | async-done | bytes 4194320 | tf_op jit(solution)/shard_map/all_gather | solution.py:165
  85.0 72.5 %all-gather.8.cloned.1.call-done = bf16[4096,512]{0,1:T(8,128)(2,1)} async-done(((bf16[128,512]{0,1:T(8,128)(2,1)}), bf16[4096,512]{0,1:T(8,128)(2,1)}) %all-gather.8.cloned.1.call-update) | async-done | bytes 4194320 | tf_op jit(solution)/shard_map/all_gather | solution.py:164
  158.3 92.3 %while.30 = (s32[]{:T(128)}, f32[512,8,64]{0,2,1:T(8,128)}, f32[512,8]{0,1:T(8,128)S(1)}, bf16[4096,512]{0,1:T(8,128)(2,1)}, pred[512,4096]{1,0:T(8,128)(4,1)}, ...) while((s32[]{:T(128)}, f32[512,8,64]{0,2,1:T(8,128)}, ...), condition=%wide.region_3.4_spmd, body=%wide.region_1.3_spmd.sunk | while | flops 558104576 | bytes 32637160 | solution.py:118
  161.6 4.5 %fusion.143 = (f32[8,512]{1,0:T(8,128)S(1)}, f32[8,512,512]{2,1,0:T(8,128)S(1)}) fusion(f32[8,512]{1,0:T(8,128)S(1)} %dynamic-slice_bitcast_fusion.4, pred[512,512]{0,1:T(8,128)(4,1)S(1)} %copy.137, bf16[512,8,64]{0,2,1:T(8,128)(2,1)S(1)} %bitcast.234, bf16[512,8,64]{0,2,1:T(8,128)(2,1)} %get-tuple-element.531), kind=kOutput, calls=%fused_computation.1.clone.1 | convolution fusion | flops 278917120 | bytes 9732096 | tf_op jit(solution)/shard_map/while/body/eval_jaxpr/thd,shd->hts/dot_general | solution.py:86
  166.1 2.6 fusion.144
  169.8 1.3 constant_dynamic-slice_fusion.10
  173.2 4.5 %fusion.143 = (f32[8,512]{1,0:T(8,128)S(1)}, f32[8,512,512]{2,1,0:T(8,128)S(1)}) fusion(f32[8,512]{1,0:T(8,128)S(1)} %dynamic-slice_bitcast_fusion.4, pred[512,512]{0,1:T(8,128)(4,1)S(1)} %copy.137, bf16[512,8,64]{0,2,1:T(8,128)(2,1)S(1)} %bitcast.234, bf16[512,8,64]{0,2,1:T(8,128)(2,1)} %get-tuple-element.531), kind=kOutput, calls=%fused_computation.1.clone.1 | convolution fusion | flops 278917120 | bytes 9732096 | tf_op jit(solution)/shard_map/while/body/eval_jaxpr/thd,shd->hts/dot_general | solution.py:86
  177.7 2.6 fusion.144
  181.4 1.3 constant_dynamic-slice_fusion.10
  184.8 4.5 %fusion.143 = (f32[8,512]{1,0:T(8,128)S(1)}, f32[8,512,512]{2,1,0:T(8,128)S(1)}) fusion(f32[8,512]{1,0:T(8,128)S(1)} %dynamic-slice_bitcast_fusion.4, pred[512,512]{0,1:T(8,128)(4,1)S(1)} %copy.137, bf16[512,8,64]{0,2,1:T(8,128)(2,1)S(1)} %bitcast.234, bf16[512,8,64]{0,2,1:T(8,128)(2,1)} %get-tuple-element.531), kind=kOutput, calls=%fused_computation.1.clone.1 | convolution fusion | flops 278917120 | bytes 9732096 | tf_op jit(solution)/shard_map/while/body/eval_jaxpr/thd,shd->hts/dot_general | solution.py:86
  189.2 2.6 fusion.144
  196.3 4.5 %fusion.143 = (f32[8,512]{1,0:T(8,128)S(1)}, f32[8,512,512]{2,1,0:T(8,128)S(1)}) fusion(f32[8,512]{1,0:T(8,128)S(1)} %dynamic-slice_bitcast_fusion.4, pred[512,512]{0,1:T(8,128)(4,1)S(1)} %copy.137, bf16[512,8,64]{0,2,1:T(8,128)(2,1)S(1)} %bitcast.234, bf16[512,8,64]{0,2,1:T(8,128)(2,1)} %get-tuple-element.531), kind=kOutput, calls=%fused_computation.1.clone.1 | convolution fusion | flops 278917120 | bytes 9732096 | tf_op jit(solution)/shard_map/while/body/eval_jaxpr/thd,shd->hts/dot_general | solution.py:86
  200.8 2.6 fusion.144
  204.4 1.3 constant_dynamic-slice_fusion.10
  207.8 4.5 %fusion.143 = (f32[8,512]{1,0:T(8,128)S(1)}, f32[8,512,512]{2,1,0:T(8,128)S(1)}) fusion(f32[8,512]{1,0:T(8,128)S(1)} %dynamic-slice_bitcast_fusion.4, pred[512,512]{0,1:T(8,128)(4,1)S(1)} %copy.137, bf16[512,8,64]{0,2,1:T(8,128)(2,1)S(1)} %bitcast.234, bf16[512,8,64]{0,2,1:T(8,128)(2,1)} %get-tuple-element.531), kind=kOutput, calls=%fused_computation.1.clone.1 | convolution fusion | flops 278917120 | bytes 9732096 | tf_op jit(solution)/shard_map/while/body/eval_jaxpr/thd,shd->hts/dot_general | solution.py:86
  212.3 2.6 fusion.144
  219.4 4.5 %fusion.143 = (f32[8,512]{1,0:T(8,128)S(1)}, f32[8,512,512]{2,1,0:T(8,128)S(1)}) fusion(f32[8,512]{1,0:T(8,128)S(1)} %dynamic-slice_bitcast_fusion.4, pred[512,512]{0,1:T(8,128)(4,1)S(1)} %copy.137, bf16[512,8,64]{0,2,1:T(8,128)(2,1)S(1)} %bitcast.234, bf16[512,8,64]{0,2,1:T(8,128)(2,1)} %get-tuple-element.531), kind=kOutput, calls=%fused_computation.1.clone.1 | convolution fusion | flops 278917120 | bytes 9732096 | tf_op jit(solution)/shard_map/while/body/eval_jaxpr/thd,shd->hts/dot_general | solution.py:86
  223.8 2.6 fusion.144
  230.9 4.5 %fusion.143 = (f32[8,512]{1,0:T(8,128)S(1)}, f32[8,512,512]{2,1,0:T(8,128)S(1)}) fusion(f32[8,512]{1,0:T(8,128)S(1)} %dynamic-slice_bitcast_fusion.4, pred[512,512]{0,1:T(8,128)(4,1)S(1)} %copy.137, bf16[512,8,64]{0,2,1:T(8,128)(2,1)S(1)} %bitcast.234, bf16[512,8,64]{0,2,1:T(8,128)(2,1)} %get-tuple-element.531), kind=kOutput, calls=%fused_computation.1.clone.1 | convolution fusion | flops 278917120 | bytes 9732096 | tf_op jit(solution)/shard_map/while/body/eval_jaxpr/thd,shd->hts/dot_general | solution.py:86
  235.4 2.6 fusion.144
  242.4 4.5 %fusion.143 = (f32[8,512]{1,0:T(8,128)S(1)}, f32[8,512,512]{2,1,0:T(8,128)S(1)}) fusion(f32[8,512]{1,0:T(8,128)S(1)} %dynamic-slice_bitcast_fusion.4, pred[512,512]{0,1:T(8,128)(4,1)S(1)} %copy.137, bf16[512,8,64]{0,2,1:T(8,128)(2,1)S(1)} %bitcast.234, bf16[512,8,64]{0,2,1:T(8,128)(2,1)} %get-tuple-element.531), kind=kOutput, calls=%fused_computation.1.clone.1 | convolution fusion | flops 278917120 | bytes 9732096 | tf_op jit(solution)/shard_map/while/body/eval_jaxpr/thd,shd->hts/dot_general | solution.py:86
  246.9 2.6 fusion.144
  250.6 12.6 %all-gather.12.cloned.1.call-done = bf16[1024,512]{1,0:T(8,128)(2,1)} async-done(((bf16[128,512]{1,0:T(8,128)(2,1)}), bf16[1024,512]{1,0:T(8,128)(2,1)}) %all-gather.12.cloned.1.call-update) | async-done | bytes 1048592 | tf_op jit(solution)/shard_map/all_gather | solution.py:173
  263.2 29.5 %while.31 = (s32[]{:T(128)}, f32[512,8,64]{0,2,1:T(8,128)}, f32[512,8]{0,1:T(8,128)S(1)}, bf16[1024,512]{1,0:T(8,128)(2,1)}, pred[512,1024]{1,0:T(8,128)(4,1)S(1...) while((s32[]{:T(128)}, f32[512,8,64]{0,2,1:T(8,128)}, ...), condition=%wide.region_6.7_spmd, body=%wide.region_4.6_spmd.sunk | while | flops 558104576 | bytes 34734312 | solution.py:118
  263.2 1.3 constant_dynamic-slice_fusion.12
  265.1 6.5 %fusion.149 = (f32[8,512]{1,0:T(8,128)S(1)}, f32[8,512,512]{2,1,0:T(8,128)}) fusion(f32[8,512]{1,0:T(8,128)S(1)} %dynamic-slice_bitcast_fusion.5, pred[512,512]{0,1:T(8,128)(4,1)S(1)} %copy.139, bf16[512,8,64]{0,2,1:T(8,128)(2,1)S(1)} %bitcast.235, bf16[512,8,64]{0,2,1:T(8,128)(2,1)} %get-tuple-element.567), kind=kOutput, calls=%fused_computation.16.clone.1 | convolution fusion | flops 278917120 | bytes 9732096 | tf_op jit(solution)/shard_map/while/body/eval_jaxpr/thd,shd->hts/dot_general | solution.py:86
  271.8 5.0 %fusion.150 = f32[512,8,64]{0,2,1:T(8,128)S(1)} fusion(f32[512,8,64]{0,2,1:T(8,128)S(1)} %copy-done.3, bf16[512,8,64]{0,2,1:T(8,128)(2,1)S(1)} %bitcast.236, f32[8,512,512]{2,1,0:T(8,128)} %get-tuple-element.499, f32[8,512]{1,0:T(8,128)S(1)} %dynamic-slice_bitcast_fusion.5, pred[512,512]{0,1:T(8,128)(4,1)S(1)} %copy.139), kind=kOutput, calls=%fused_computation.21.clone.1 | convolution fusion | flops 279183360 | bytes 11288576 | tf_op jit(solution)/shard_map/while/body/eval_jaxpr/hts,shd->thd/dot_general | solution.py:96
  279.9 6.5 %fusion.149 = (f32[8,512]{1,0:T(8,128)S(1)}, f32[8,512,512]{2,1,0:T(8,128)}) fusion(f32[8,512]{1,0:T(8,128)S(1)} %dynamic-slice_bitcast_fusion.5, pred[512,512]{0,1:T(8,128)(4,1)S(1)} %copy.139, bf16[512,8,64]{0,2,1:T(8,128)(2,1)S(1)} %bitcast.235, bf16[512,8,64]{0,2,1:T(8,128)(2,1)} %get-tuple-element.567), kind=kOutput, calls=%fused_computation.16.clone.1 | convolution fusion | flops 278917120 | bytes 9732096 | tf_op jit(solution)/shard_map/while/body/eval_jaxpr/thd,shd->hts/dot_general | solution.py:86
  286.6 5.0 %fusion.150 = f32[512,8,64]{0,2,1:T(8,128)S(1)} fusion(f32[512,8,64]{0,2,1:T(8,128)S(1)} %copy-done.3, bf16[512,8,64]{0,2,1:T(8,128)(2,1)S(1)} %bitcast.236, f32[8,512,512]{2,1,0:T(8,128)} %get-tuple-element.499, f32[8,512]{1,0:T(8,128)S(1)} %dynamic-slice_bitcast_fusion.5, pred[512,512]{0,1:T(8,128)(4,1)S(1)} %copy.139), kind=kOutput, calls=%fused_computation.21.clone.1 | convolution fusion | flops 279183360 | bytes 11288576 | tf_op jit(solution)/shard_map/while/body/eval_jaxpr/hts,shd->thd/dot_general | solution.py:96
  292.6 3.4 %fusion.40 = bf16[512,8,64]{0,2,1:T(8,128)(2,1)S(1)} fusion(f32[512,8,64]{0,2,1:T(8,128)} %get-tuple-element.287, f32[512,8]{0,1:T(8,128)S(1)} %get-tuple-element.288), kind=kLoop, calls=%fused_computation.59 | loop fusion | flops 17301504 | bytes 1589248 | tf_op jit(solution)/shard_map/convert_element_type | solution.py:181
  296.1 1.6 fusion.100
  (154 shorter events, 50.5 us)
Async XLA Ops:
  6.5 289.5 %copy-start = (bf16[512,512]{1,0:T(8,128)(2,1)S(1)}, bf16[512,512]{1,0:T(8,128)(2,1)}, u32[]{:S(2)}) copy-start(bf16[512,512]{1,0:T(8,128)(2,1)} %param.33) | copy-start | bytes 1572868
  6.5 22.7 %copy-start.6 = (bf16[512,512]{1,0:T(8,128)(2,1)S(1)}, bf16[512,512]{1,0:T(8,128)(2,1)}, u32[]{:S(2)}) copy-start(bf16[512,512]{1,0:T(8,128)(2,1)} %param.23) | copy-start | bytes 1572868
  6.5 28.4 %copy-start.11 = (f32[4,8]{1,0:T(4,128)S(1)}, f32[4,8]{1,0:T(4,128)}, u32[]{:S(2)}) copy-start(f32[4,8]{1,0:T(4,128)} %param.32) | copy-start | bytes 388
  6.5 78.5 %all-gather.6.cloned.1.call-start = ((), (), s32[]{:S(2)}) async-start(), calls=%async_computation | async-start | bytes 4325376 | tf_op jit(solution)/shard_map/all_gather | solution.py:165
  9.9 28.3 %copy-start.7 = (s32[4,8,128,128]{3,2,1,0:T(8,128)S(1)}, s32[4,8,128,128]{3,2,1,0:T(8,128)}, u32[]{:S(2)}) copy-start(s32[4,8,128,128]{3,2,1,0:T(8,128)} %param.36) | copy-start | bytes 6291460
  9.9 147.6 %all-gather.8.cloned.1.call-start = ((), (), s32[]{:S(2)}) async-start(), calls=%async_computation.1 | async-start | bytes 4325376 | tf_op jit(solution)/shard_map/all_gather | solution.py:164
  13.4 237.2 %all-gather.10.cloned.1.call-start = ((), (), s32[]{:S(2)}) async-start(), calls=%async_computation.2 | async-start | bytes 1179648 | tf_op jit(solution)/shard_map/all_gather | solution.py:174
  28.6 234.5 %all-gather.12.cloned.1.call-start = ((), (), s32[]{:S(2)}) async-start(), calls=%async_computation.3 | async-start | bytes 1179648 | tf_op jit(solution)/shard_map/all_gather | solution.py:173
  36.5 1.7 copy-start.5
  39.2 5.6 %copy-start.13 = (s32[128]{0:T(128)S(1)}, s32[128]{0:T(128)}, u32[]{:S(2)}) copy-start(s32[128]{0:T(128)} %param.26) | copy-start | bytes 1540
  39.2 29.0 %copy-start.8 = (s32[4,2,128,128]{3,2,1,0:T(8,128)S(1)}, s32[4,2,128,128]{3,2,1,0:T(8,128)}, u32[]{:S(2)}) copy-start(s32[4,2,128,128]{3,2,1,0:T(8,128)} %param.39) | copy-start | bytes 1572868
  39.2 29.1 %copy-start.12 = (s32[4,2]{0,1:T(2,128)S(1)}, s32[4,2]{0,1:T(2,128)}, u32[]{:S(2)}) copy-start(s32[4,2]{0,1:T(2,128)} %param.40) | copy-start | bytes 100
  39.2 29.2 %copy-start.14 = (s32[4,2]{0,1:T(2,128)S(1)}, s32[4,2]{0,1:T(2,128)}, u32[]{:S(2)}) copy-start(s32[4,2]{0,1:T(2,128)} %param.41) | copy-start | bytes 100
  41.7 28.5 %copy-start.9 = (bf16[512,512]{0,1:T(8,128)(2,1)S(1)}, bf16[512,512]{0,1:T(8,128)(2,1)}, u32[]{:S(2)}) copy-start(bf16[512,512]{0,1:T(8,128)(2,1)} %convolution_convert_fusion.2) | copy-start | bytes 1572868
  161.6 4.5 %copy-start.1 = (f32[512,8,64]{0,2,1:T(8,128)S(1)}, f32[512,8,64]{0,2,1:T(8,128)}, u32[]{:S(2)}) copy-start(f32[512,8,64]{0,2,1:T(8,128)} %get-tuple-element.514) | copy-start | bytes 3145732 | tf_op jit(solution)/shard_map/while
  168.8 1.0 copy-start.2
  173.2 4.5 %copy-start.1 = (f32[512,8,64]{0,2,1:T(8,128)S(1)}, f32[512,8,64]{0,2,1:T(8,128)}, u32[]{:S(2)}) copy-start(f32[512,8,64]{0,2,1:T(8,128)} %get-tuple-element.514) | copy-start | bytes 3145732 | tf_op jit(solution)/shard_map/while
  180.3 1.0 copy-start.2
  184.8 4.5 %copy-start.1 = (f32[512,8,64]{0,2,1:T(8,128)S(1)}, f32[512,8,64]{0,2,1:T(8,128)}, u32[]{:S(2)}) copy-start(f32[512,8,64]{0,2,1:T(8,128)} %get-tuple-element.514) | copy-start | bytes 3145732 | tf_op jit(solution)/shard_map/while
  191.9 1.0 copy-start.2
  196.3 4.5 %copy-start.1 = (f32[512,8,64]{0,2,1:T(8,128)S(1)}, f32[512,8,64]{0,2,1:T(8,128)}, u32[]{:S(2)}) copy-start(f32[512,8,64]{0,2,1:T(8,128)} %get-tuple-element.514) | copy-start | bytes 3145732 | tf_op jit(solution)/shard_map/while
  203.4 1.0 copy-start.2
  207.8 4.5 %copy-start.1 = (f32[512,8,64]{0,2,1:T(8,128)S(1)}, f32[512,8,64]{0,2,1:T(8,128)}, u32[]{:S(2)}) copy-start(f32[512,8,64]{0,2,1:T(8,128)} %get-tuple-element.514) | copy-start | bytes 3145732 | tf_op jit(solution)/shard_map/while
  215.0 1.0 copy-start.2
  219.4 4.5 %copy-start.1 = (f32[512,8,64]{0,2,1:T(8,128)S(1)}, f32[512,8,64]{0,2,1:T(8,128)}, u32[]{:S(2)}) copy-start(f32[512,8,64]{0,2,1:T(8,128)} %get-tuple-element.514) | copy-start | bytes 3145732 | tf_op jit(solution)/shard_map/while
  226.5 1.0 copy-start.2
  230.9 4.5 %copy-start.1 = (f32[512,8,64]{0,2,1:T(8,128)S(1)}, f32[512,8,64]{0,2,1:T(8,128)}, u32[]{:S(2)}) copy-start(f32[512,8,64]{0,2,1:T(8,128)} %get-tuple-element.514) | copy-start | bytes 3145732 | tf_op jit(solution)/shard_map/while
  238.0 1.0 copy-start.2
  242.4 4.5 %copy-start.1 = (f32[512,8,64]{0,2,1:T(8,128)S(1)}, f32[512,8,64]{0,2,1:T(8,128)}, u32[]{:S(2)}) copy-start(f32[512,8,64]{0,2,1:T(8,128)} %get-tuple-element.514) | copy-start | bytes 3145732 | tf_op jit(solution)/shard_map/while
  249.6 1.0 copy-start.2
  263.2 34.7 %copy-start.10 = (f32[512]{0:T(512)S(1)}, f32[512]{0:T(512)}, u32[]{:S(2)}) copy-start(f32[512]{0:T(512)} %param.35) | copy-start | bytes 6148
  265.1 6.7 %copy-start.3 = (f32[512,8,64]{0,2,1:T(8,128)S(1)}, f32[512,8,64]{0,2,1:T(8,128)}, u32[]{:S(2)}) copy-start(f32[512,8,64]{0,2,1:T(8,128)} %get-tuple-element.550) | copy-start | bytes 3145732 | tf_op jit(solution)/shard_map/while
  276.9 1.0 copy-start.4
  279.8 6.7 %copy-start.3 = (f32[512,8,64]{0,2,1:T(8,128)S(1)}, f32[512,8,64]{0,2,1:T(8,128)}, u32[]{:S(2)}) copy-start(f32[512,8,64]{0,2,1:T(8,128)} %get-tuple-element.550) | copy-start | bytes 3145732 | tf_op jit(solution)/shard_map/while
  291.6 1.0 copy-start.4
Sparse Core Ops, SparseCore 0:
  10.0 74.9 all-gather.5
  86.8 70.6 all-gather.7
  160.2 50.1 all-gather.9
  212.8 50.2 all-gather.11
where the time goes:
time: 307 us; the launch traced here: 306 us
  matrix products  111 us (36%)
  waiting for transfers between devices  98.1 us (32%)
  local copies, waits for them, and re-layouts  50.6 us (16%)
  blocking collectives  23.5 us (8%)
  between operations  14.1 us (5%)
  other arithmetic  7.42 us (2%)
    all_gather x1, waiting for transfers between devices, per_device(): key_rows = lax.all_gather(cite_keys, 'paper', axis=0, tiled=True)  72.5 us
    dot_general x10, matrix products, attend(): jnp.einsum('thd,shd->hts', query_heads, head_split(key_rows, head_count),...  48.6 us
    dot_general x10, matrix products, attend(): jnp.einsum('hts,shd->thd', weights.astype(jnp.bfloat16), head_split(value...  31.2 us
    all_gather x1, blocking collectives, per_device(): kind_ids = lax.all_gather(entity_kinds, 'type', axis=0, tiled=True)  23.5 us
    dynamic_slice x12, local copies, waits for them, and re-layouts, single_block(): part_keys = lax.dynamic_slice_in_dim(key_rows, offset, block_rows, 0)  13.2 us
    all_gather x1, waiting for transfers between devices, per_device(): key_rows = lax.all_gather(entity_keys, 'type', axis=0, tiled=True)  12.6 us
    all_gather x1, waiting for transfers between devices, per_device(): value_rows = lax.all_gather(cite_values, 'paper', axis=0, tiled=True)  12.5 us
    dot_general x8, matrix products, relate(): jnp.einsum('nhd,hde->nhe', head_split(raw_rows, head_count), weight, pref...  12 us
  transfers between devices with their start and end apart: 4, of which 3 were waited for; matrix products, arithmetic and copies ran while one was open for 40% of the time, Pallas kernels for 0%

commit v1 on v0

--- a/solution.py
+++ b/solution.py
@@ -162,7 +162,8 @@
         cited_rows, key_weight, value_weight, attention_rel, message_rel
     )
     key_rows = lax.all_gather(cite_keys, "paper", axis=0, tiled=True)
-    value_rows = lax.all_gather(cite_values, "paper", axis=0, tiled=True)
+    sent = jnp.stack([cite_values] * lax.axis_size("paper"))
+    value_rows = jnp.concatenate(lax.all_to_all(sent, "paper", 0, 0), axis=0)
     row_count = key_rows.shape[0]
     scales = jnp.broadcast_to(cite_scale[None, :], (row_count, head_count))
     live_mask = cite_live

time: 307 us -> 320 us (1.042)
  waiting for transfers between devices: 98.1 us -> 67 us
  matrix products: 111 us -> 136 us
  starting transfers between devices: 0.13 us -> 9.93 us
  local copies, waits for them, and re-layouts: 50.6 us -> 58.6 us
    all_gather x1, waiting for transfers between devices: 72.5 us -> 0.01 us  [per_device(): key_rows = lax.all_gather(cite_keys, 'paper', axis=0, tiled=True)]
    all_to_all x0 -> x1, waiting for transfers between devices: none -> 66.2 us  [per_device(): value_rows = jnp.concatenate(lax.all_to_all(sent, 'paper', 0, 0), axis=0)]
    dot_general x10, matrix products: 31.2 us -> 50.4 us  [attend(): jnp.einsum('hts,shd->thd', weights.astype(jnp.bfloat16), head_split(value...]
    dot_general x10, matrix products: 48.6 us -> 64 us  [attend(): jnp.einsum('thd,shd->hts', query_heads, head_split(key_rows, head_count),...]
    all_gather x1, waiting for transfers between devices: 12.6 us -> 0.02 us  [per_device(): key_rows = lax.all_gather(entity_keys, 'type', axis=0, tiled=True)]
    all_gather x1 -> x0, waiting for transfers between devices: 12.5 us -> none  [per_device(): value_rows = lax.all_gather(cite_values, 'paper', axis=0, tiled=True)]
    dynamic_slice x2 -> x18, local copies, waits for them, and re-layouts: 0.42 us -> 10.7 us  [single_block(): part_values = lax.dynamic_slice_in_dim(value_rows, offset, block_rows, 0)]
    all_to_all x0 -> x1, starting transfers between devices: none -> 9.84 us  [per_device(): value_rows = jnp.concatenate(lax.all_to_all(sent, 'paper', 0, 0), axis=0)]
  transfers between devices with their start and end apart: 4 -> 4, of which waited for: 3 -> 1; matrix products, arithmetic and copies ran while one was open for 40% -> 51% of each run, Pallas kernels for 0% -> 0%
where the time goes in v1:
time: 320 us; the launch traced here: 316 us
  matrix products  136 us (42%)
  waiting for transfers between devices  67 us (21%)
  local copies, waits for them, and re-layouts  58.6 us (18%)
  blocking collectives  23.4 us (7%)
  between operations  14.3 us (4%)
  starting transfers between devices  9.93 us (3%)
  other arithmetic  5.61 us (2%)
    all_to_all x1, waiting for transfers between devices, per_device(): value_rows = jnp.concatenate(lax.all_to_all(sent, 'paper', 0, 0), axis=0)  66.2 us
    dot_general x10, matrix products, attend(): jnp.einsum('thd,shd->hts', query_heads, head_split(key_rows, head_count),...  64 us
    dot_general x10, matrix products, attend(): jnp.einsum('hts,shd->thd', weights.astype(jnp.bfloat16), head_split(value...  50.4 us
    all_gather x1, blocking collectives, per_device(): kind_ids = lax.all_gather(entity_kinds, 'type', axis=0, tiled=True)  23.4 us
    dynamic_slice x20, local copies, waits for them, and re-layouts, single_block(): part_live = lax.dynamic_slice_in_dim(live_mask, offset, block_rows, 1)  11.8 us
    dynamic_slice x12, local copies, waits for them, and re-layouts, single_block(): part_keys = lax.dynamic_slice_in_dim(key_rows, offset, block_rows, 0)  11.6 us
    dynamic_slice x18, local copies, waits for them, and re-layouts, single_block(): part_values = lax.dynamic_slice_in_dim(value_rows, offset, block_rows, 0)  10.7 us
    all_to_all x1, starting transfers between devices, per_device(): value_rows = jnp.concatenate(lax.all_to_all(sent, 'paper', 0, 0), axis=0)  9.84 us
  transfers between devices with their start and end apart: 4, of which 1 were waited for; matrix products, arithmetic and copies ran while one was open for 51% of the time, Pallas kernels for 0%

profile of v1, /device:TPU:32, one launch (start us, length us, event | category | flops | bytes accessed | tf_op | source)
XLA Modules:
  0.0 315.6 jit_solution(1327201334112478297)
XLA Ops:
  6.5 1.4 convolution_convert_fusion.5
  8.1 1.8 convolution_convert_fusion.7
  10.0 1.3 convolution_convert_fusion.6
  11.4 1.1 convolution_convert_fusion.8
  12.6 2.9 stack.2
  15.5 9.8 %all-to-all-start = ((bf16[32,128,512]{1,2,0:T(8,128)(2,1)}), bf16[32,128,512]{1,2,0:T(8,128)(2,1)}, u32[]{:S(2)}, u32[]{:S(2)}) async-start(bf16[32,128,512]{1,2,0:T(8,128)(2,1)} %stack.2), calls=%async_computation | async-start | bytes 8388608 | tf_op jit(solution)/shard_map/all_to_all | solution.py:166
  25.5 1.3 fusion.53
  26.8 1.3 fusion.36
  28.9 1.3 fusion.50
  30.2 1.3 fusion.37
  34.9 1.5 convolution_convert_fusion.3
  36.4 1.3 convolution_convert_fusion.4
  37.7 1.4 fusion.35
  39.3 1.8 convert_element_type.128
  41.1 1.8 broadcast_compare_fusion
  42.9 2.9 copy.163
  47.8 23.4 %all-gather = s32[8,1,128]{2,1,0:T(1,128)S(1)} all-gather(s32[1,1,128]{2,1,0:T(1,128)S(1)} %bitcast.259), channel_id=1, replica_groups=mesh['paper'=32,'type'=8] {'type'}, dimensions={0}, use_global_device_ids=true | all-gather | bytes 4608 | tf_op jit(solution)/shard_map/all_gather | solution.py:176
  71.2 1.5 convolution_convert_fusion.2
  73.1 66.2 %all-to-all-done = bf16[32,128,512]{1,2,0:T(8,128)(2,1)} async-done(((bf16[32,128,512]{1,2,0:T(8,128)(2,1)}), bf16[32,128,512]{1,2,0:T(8,128)(2,1)}, u32[]{:S(2)}, u32[]{:S(2)}) %all-to-all-start) | async-done | bytes 4194336 | tf_op jit(solution)/shard_map/all_to_all | solution.py:166
  139.3 6.5 %copy.113 = bf16[32,128,512]{2,1,0:T(8,128)(2,1)} copy(bf16[32,128,512]{1,2,0:T(8,128)(2,1)} %all-to-all-done) | data formatting | bytes 8388608 | tf_op jit(solution)/shard_map/all_to_all | solution.py:166
  146.5 127.6 %while.30 = (s32[]{:T(128)}, f32[512,8,64]{0,2,1:T(8,128)S(1)}, f32[512,8]{0,1:T(8,128)S(1)}, bf16[4096,512]{1,0:T(8,128)(2,1)}, pred[512,4096]{1,0:T(8,128)(4,1...) while((s32[]{:T(128)}, f32[512,8,64]{0,2,1:T(8,128)S(1)}, ...), condition=%wide.region_3.4_spmd, body=%wide.region_1.3_spmd.sunk | while | flops 558104576 | bytes 25297076 | solution.py:118
  149.7 6.4 %fusion.143 = (f32[8,512]{1,0:T(8,128)S(1)}, f32[8,512,512]{2,1,0:T(8,128)}) fusion(f32[8,512]{1,0:T(8,128)S(1)} %dynamic-slice_bitcast_fusion.4, pred[512,512]{0,1:T(8,128)(4,1)S(1)} %copy.171, bf16[512,8,64]{0,2,1:T(8,128)(2,1)S(1)} %bitcast.237, bf16[512,8,64]{0,2,1:T(8,128)(2,1)} %get-tuple-element.541), kind=kOutput, calls=%fused_computation.1.clone.1 | convolution fusion | flops 278917120 | bytes 9732096 | tf_op jit(solution)/shard_map/while/body/eval_jaxpr/thd,shd->hts/dot_general | solution.py:86
  157.4 5.1 %fusion.144 = f32[512,8,64]{0,2,1:T(8,128)S(1)} fusion(f32[512,8,64]{0,2,1:T(8,128)S(1)} %get-tuple-element.524, bf16[512,8,64]{0,2,1:T(8,128)(2,1)S(1)} %bitcast.235, f32[8,512,512]{2,1,0:T(8,128)} %get-tuple-element.497, f32[8,512]{1,0:T(8,128)S(1)} %dynamic-slice_bitcast_fusion.4, pred[512,512]{0,1:T(8,128)(4,1)S(1)} %copy.171), kind=kOutput, calls=%fused_computation.6.clone.1 | convolution fusion | flops 279183360 | bytes 11288576 | tf_op jit(solution)/shard_map/while/body/eval_jaxpr/hts,shd->thd/dot_general | solution.py:96
  165.7 6.4 %fusion.143 = (f32[8,512]{1,0:T(8,128)S(1)}, f32[8,512,512]{2,1,0:T(8,128)}) fusion(f32[8,512]{1,0:T(8,128)S(1)} %dynamic-slice_bitcast_fusion.4, pred[512,512]{0,1:T(8,128)(4,1)S(1)} %copy.171, bf16[512,8,64]{0,2,1:T(8,128)(2,1)S(1)} %bitcast.237, bf16[512,8,64]{0,2,1:T(8,128)(2,1)} %get-tuple-element.541), kind=kOutput, calls=%fused_computation.1.clone.1 | convolution fusion | flops 278917120 | bytes 9732096 | tf_op jit(solution)/shard_map/while/body/eval_jaxpr/thd,shd->hts/dot_general | solution.py:86
  173.4 5.0 %fusion.144 = f32[512,8,64]{0,2,1:T(8,128)S(1)} fusion(f32[512,8,64]{0,2,1:T(8,128)S(1)} %get-tuple-element.524, bf16[512,8,64]{0,2,1:T(8,128)(2,1)S(1)} %bitcast.235, f32[8,512,512]{2,1,0:T(8,128)} %get-tuple-element.497, f32[8,512]{1,0:T(8,128)S(1)} %dynamic-slice_bitcast_fusion.4, pred[512,512]{0,1:T(8,128)(4,1)S(1)} %copy.171), kind=kOutput, calls=%fused_computation.6.clone.1 | convolution fusion | flops 279183360 | bytes 11288576 | tf_op jit(solution)/shard_map/while/body/eval_jaxpr/hts,shd->thd/dot_general | solution.py:96
  181.6 6.4 %fusion.143 = (f32[8,512]{1,0:T(8,128)S(1)}, f32[8,512,512]{2,1,0:T(8,128)}) fusion(f32[8,512]{1,0:T(8,128)S(1)} %dynamic-slice_bitcast_fusion.4, pred[512,512]{0,1:T(8,128)(4,1)S(1)} %copy.171, bf16[512,8,64]{0,2,1:T(8,128)(2,1)S(1)} %bitcast.237, bf16[512,8,64]{0,2,1:T(8,128)(2,1)} %get-tuple-element.541), kind=kOutput, calls=%fused_computation.1.clone.1 | convolution fusion | flops 278917120 | bytes 9732096 | tf_op jit(solution)/shard_map/while/body/eval_jaxpr/thd,shd->hts/dot_general | solution.py:86
  188.0 1.1 constant_dynamic-slice_fusion.11
  189.3 5.0 %fusion.144 = f32[512,8,64]{0,2,1:T(8,128)S(1)} fusion(f32[512,8,64]{0,2,1:T(8,128)S(1)} %get-tuple-element.524, bf16[512,8,64]{0,2,1:T(8,128)(2,1)S(1)} %bitcast.235, f32[8,512,512]{2,1,0:T(8,128)} %get-tuple-element.497, f32[8,512]{1,0:T(8,128)S(1)} %dynamic-slice_bitcast_fusion.4, pred[512,512]{0,1:T(8,128)(4,1)S(1)} %copy.171), kind=kOutput, calls=%fused_computation.6.clone.1 | convolution fusion | flops 279183360 | bytes 11288576 | tf_op jit(solution)/shard_map/while/body/eval_jaxpr/hts,shd->thd/dot_general | solution.py:96
  197.6 6.4 %fusion.143 = (f32[8,512]{1,0:T(8,128)S(1)}, f32[8,512,512]{2,1,0:T(8,128)}) fusion(f32[8,512]{1,0:T(8,128)S(1)} %dynamic-slice_bitcast_fusion.4, pred[512,512]{0,1:T(8,128)(4,1)S(1)} %copy.171, bf16[512,8,64]{0,2,1:T(8,128)(2,1)S(1)} %bitcast.237, bf16[512,8,64]{0,2,1:T(8,128)(2,1)} %get-tuple-element.541), kind=kOutput, calls=%fused_computation.1.clone.1 | convolution fusion | flops 278917120 | bytes 9732096 | tf_op jit(solution)/shard_map/while/body/eval_jaxpr/thd,shd->hts/dot_general | solution.py:86
  205.3 5.0 %fusion.144 = f32[512,8,64]{0,2,1:T(8,128)S(1)} fusion(f32[512,8,64]{0,2,1:T(8,128)S(1)} %get-tuple-element.524, bf16[512,8,64]{0,2,1:T(8,128)(2,1)S(1)} %bitcast.235, f32[8,512,512]{2,1,0:T(8,128)} %get-tuple-element.497, f32[8,512]{1,0:T(8,128)S(1)} %dynamic-slice_bitcast_fusion.4, pred[512,512]{0,1:T(8,128)(4,1)S(1)} %copy.171), kind=kOutput, calls=%fused_computation.6.clone.1 | convolution fusion | flops 279183360 | bytes 11288576 | tf_op jit(solution)/shard_map/while/body/eval_jaxpr/hts,shd->thd/dot_general | solution.py:96
  212.5 1.1 constant_dynamic-slice_fusion.13
  213.5 6.4 %fusion.143 = (f32[8,512]{1,0:T(8,128)S(1)}, f32[8,512,512]{2,1,0:T(8,128)}) fusion(f32[8,512]{1,0:T(8,128)S(1)} %dynamic-slice_bitcast_fusion.4, pred[512,512]{0,1:T(8,128)(4,1)S(1)} %copy.171, bf16[512,8,64]{0,2,1:T(8,128)(2,1)S(1)} %bitcast.237, bf16[512,8,64]{0,2,1:T(8,128)(2,1)} %get-tuple-element.541), kind=kOutput, calls=%fused_computation.1.clone.1 | convolution fusion | flops 278917120 | bytes 9732096 | tf_op jit(solution)/shard_map/while/body/eval_jaxpr/thd,shd->hts/dot_general | solution.py:86
  221.2 5.0 %fusion.144 = f32[512,8,64]{0,2,1:T(8,128)S(1)} fusion(f32[512,8,64]{0,2,1:T(8,128)S(1)} %get-tuple-element.524, bf16[512,8,64]{0,2,1:T(8,128)(2,1)S(1)} %bitcast.235, f32[8,512,512]{2,1,0:T(8,128)} %get-tuple-element.497, f32[8,512]{1,0:T(8,128)S(1)} %dynamic-slice_bitcast_fusion.4, pred[512,512]{0,1:T(8,128)(4,1)S(1)} %copy.171), kind=kOutput, calls=%fused_computation.6.clone.1 | convolution fusion | flops 279183360 | bytes 11288576 | tf_op jit(solution)/shard_map/while/body/eval_jaxpr/hts,shd->thd/dot_general | solution.py:96
  229.5 6.4 %fusion.143 = (f32[8,512]{1,0:T(8,128)S(1)}, f32[8,512,512]{2,1,0:T(8,128)}) fusion(f32[8,512]{1,0:T(8,128)S(1)} %dynamic-slice_bitcast_fusion.4, pred[512,512]{0,1:T(8,128)(4,1)S(1)} %copy.171, bf16[512,8,64]{0,2,1:T(8,128)(2,1)S(1)} %bitcast.237, bf16[512,8,64]{0,2,1:T(8,128)(2,1)} %get-tuple-element.541), kind=kOutput, calls=%fused_computation.1.clone.1 | convolution fusion | flops 278917120 | bytes 9732096 | tf_op jit(solution)/shard_map/while/body/eval_jaxpr/thd,shd->hts/dot_general | solution.py:86
  237.2 5.0 %fusion.144 = f32[512,8,64]{0,2,1:T(8,128)S(1)} fusion(f32[512,8,64]{0,2,1:T(8,128)S(1)} %get-tuple-element.524, bf16[512,8,64]{0,2,1:T(8,128)(2,1)S(1)} %bitcast.235, f32[8,512,512]{2,1,0:T(8,128)} %get-tuple-element.497, f32[8,512]{1,0:T(8,128)S(1)} %dynamic-slice_bitcast_fusion.4, pred[512,512]{0,1:T(8,128)(4,1)S(1)} %copy.171), kind=kOutput, calls=%fused_computation.6.clone.1 | convolution fusion | flops 279183360 | bytes 11288576 | tf_op jit(solution)/shard_map/while/body/eval_jaxpr/hts,shd->thd/dot_general | solution.py:96
  245.4 6.4 %fusion.143 = (f32[8,512]{1,0:T(8,128)S(1)}, f32[8,512,512]{2,1,0:T(8,128)}) fusion(f32[8,512]{1,0:T(8,128)S(1)} %dynamic-slice_bitcast_fusion.4, pred[512,512]{0,1:T(8,128)(4,1)S(1)} %copy.171, bf16[512,8,64]{0,2,1:T(8,128)(2,1)S(1)} %bitcast.237, bf16[512,8,64]{0,2,1:T(8,128)(2,1)} %get-tuple-element.541), kind=kOutput, calls=%fused_computation.1.clone.1 | convolution fusion | flops 278917120 | bytes 9732096 | tf_op jit(solution)/shard_map/while/body/eval_jaxpr/thd,shd->hts/dot_general | solution.py:86
  253.1 5.0 %fusion.144 = f32[512,8,64]{0,2,1:T(8,128)S(1)} fusion(f32[512,8,64]{0,2,1:T(8,128)S(1)} %get-tuple-element.524, bf16[512,8,64]{0,2,1:T(8,128)(2,1)S(1)} %bitcast.235, f32[8,512,512]{2,1,0:T(8,128)} %get-tuple-element.497, f32[8,512]{1,0:T(8,128)S(1)} %dynamic-slice_bitcast_fusion.4, pred[512,512]{0,1:T(8,128)(4,1)S(1)} %copy.171), kind=kOutput, calls=%fused_computation.6.clone.1 | convolution fusion | flops 279183360 | bytes 11288576 | tf_op jit(solution)/shard_map/while/body/eval_jaxpr/hts,shd->thd/dot_general | solution.py:96
  261.4 6.4 %fusion.143 = (f32[8,512]{1,0:T(8,128)S(1)}, f32[8,512,512]{2,1,0:T(8,128)}) fusion(f32[8,512]{1,0:T(8,128)S(1)} %dynamic-slice_bitcast_fusion.4, pred[512,512]{0,1:T(8,128)(4,1)S(1)} %copy.171, bf16[512,8,64]{0,2,1:T(8,128)(2,1)S(1)} %bitcast.237, bf16[512,8,64]{0,2,1:T(8,128)(2,1)} %get-tuple-element.541), kind=kOutput, calls=%fused_computation.1.clone.1 | convolution fusion | flops 278917120 | bytes 9732096 | tf_op jit(solution)/shard_map/while/body/eval_jaxpr/thd,shd->hts/dot_general | solution.py:86
  269.1 5.0 %fusion.144 = f32[512,8,64]{0,2,1:T(8,128)S(1)} fusion(f32[512,8,64]{0,2,1:T(8,128)S(1)} %get-tuple-element.524, bf16[512,8,64]{0,2,1:T(8,128)(2,1)S(1)} %bitcast.235, f32[8,512,512]{2,1,0:T(8,128)} %get-tuple-element.497, f32[8,512]{1,0:T(8,128)S(1)} %dynamic-slice_bitcast_fusion.4, pred[512,512]{0,1:T(8,128)(4,1)S(1)} %copy.171), kind=kOutput, calls=%fused_computation.6.clone.1 | convolution fusion | flops 279183360 | bytes 11288576 | tf_op jit(solution)/shard_map/while/body/eval_jaxpr/hts,shd->thd/dot_general | solution.py:96
  274.2 29.6 %while.31 = (s32[]{:T(128)}, f32[512,8,64]{0,2,1:T(8,128)S(1)}, f32[512,8]{0,1:T(8,128)S(1)}, bf16[1024,512]{1,0:T(8,128)(2,1)}, pred[512,1024]{1,0:T(8,128)(4,1...) while((s32[]{:T(128)}, f32[512,8,64]{0,2,1:T(8,128)S(1)}, ...), condition=%wide.region_6.7_spmd, body=%wide.region_4.6_spmd.sunk | while | flops 558104576 | bytes 34734312 | solution.py:118
  275.3 1.3 constant_dynamic-slice_fusion.14
  277.2 6.5 %fusion.149 = (f32[8,512]{1,0:T(8,128)S(1)}, f32[8,512,512]{2,1,0:T(8,128)}) fusion(f32[8,512]{1,0:T(8,128)S(1)} %dynamic-slice_bitcast_fusion.5, pred[512,512]{0,1:T(8,128)(4,1)S(1)} %copy.173, bf16[512,8,64]{0,2,1:T(8,128)(2,1)S(1)} %bitcast.234, bf16[512,8,64]{0,2,1:T(8,128)(2,1)} %get-tuple-element.577), kind=kOutput, calls=%fused_computation.16.clone.1 | convolution fusion | flops 278917120 | bytes 9732096 | tf_op jit(solution)/shard_map/while/body/eval_jaxpr/thd,shd->hts/dot_general | solution.py:86
  283.9 5.0 %fusion.150 = f32[512,8,64]{0,2,1:T(8,128)S(1)} fusion(f32[512,8,64]{0,2,1:T(8,128)S(1)} %copy-done.2, bf16[512,8,64]{0,2,1:T(8,128)(2,1)S(1)} %bitcast.236, f32[8,512,512]{2,1,0:T(8,128)} %get-tuple-element.509, f32[8,512]{1,0:T(8,128)S(1)} %dynamic-slice_bitcast_fusion.5, pred[512,512]{0,1:T(8,128)(4,1)S(1)} %copy.173), kind=kOutput, calls=%fused_computation.21.clone.1 | convolution fusion | flops 279183360 | bytes 11288576 | tf_op jit(solution)/shard_map/while/body/eval_jaxpr/hts,shd->thd/dot_general | solution.py:96
  290.1 1.3 constant_dynamic-slice_fusion.14
  292.0 6.5 %fusion.149 = (f32[8,512]{1,0:T(8,128)S(1)}, f32[8,512,512]{2,1,0:T(8,128)}) fusion(f32[8,512]{1,0:T(8,128)S(1)} %dynamic-slice_bitcast_fusion.5, pred[512,512]{0,1:T(8,128)(4,1)S(1)} %copy.173, bf16[512,8,64]{0,2,1:T(8,128)(2,1)S(1)} %bitcast.234, bf16[512,8,64]{0,2,1:T(8,128)(2,1)} %get-tuple-element.577), kind=kOutput, calls=%fused_computation.16.clone.1 | convolution fusion | flops 278917120 | bytes 9732096 | tf_op jit(solution)/shard_map/while/body/eval_jaxpr/thd,shd->hts/dot_general | solution.py:86
  298.7 5.0 %fusion.150 = f32[512,8,64]{0,2,1:T(8,128)S(1)} fusion(f32[512,8,64]{0,2,1:T(8,128)S(1)} %copy-done.2, bf16[512,8,64]{0,2,1:T(8,128)(2,1)S(1)} %bitcast.236, f32[8,512,512]{2,1,0:T(8,128)} %get-tuple-element.509, f32[8,512]{1,0:T(8,128)S(1)} %dynamic-slice_bitcast_fusion.5, pred[512,512]{0,1:T(8,128)(4,1)S(1)} %copy.173), kind=kOutput, calls=%fused_computation.21.clone.1 | convolution fusion | flops 279183360 | bytes 11288576 | tf_op jit(solution)/shard_map/while/body/eval_jaxpr/hts,shd->thd/dot_general | solution.py:96
  303.8 2.4 fusion.40
  306.2 1.6 fusion.100
  (145 shorter events, 45.8 us)
Async XLA Ops:
  6.5 299.6 %copy-start = (bf16[512,512]{1,0:T(8,128)(2,1)S(1)}, bf16[512,512]{1,0:T(8,128)(2,1)}, u32[]{:S(2)}) copy-start(bf16[512,512]{1,0:T(8,128)(2,1)} %param.33) | copy-start | bytes 1572868
  6.5 18.9 %copy-start.12 = (s32[128]{0:T(128)S(1)}, s32[128]{0:T(128)}, u32[]{:S(2)}) copy-start(s32[128]{0:T(128)} %param.26) | copy-start | bytes 1540
  6.5 19.0 %copy-start.13 = (bf16[128,512]{1,0:T(8,128)(2,1)S(1)}, bf16[128,512]{1,0:T(8,128)(2,1)}, u32[]{:S(2)}) copy-start(bf16[128,512]{1,0:T(8,128)(2,1)} %param.25) | copy-start | bytes 393220
  6.5 139.3 %all-gather.5.cloned.1.call-start = ((), (), s32[]{:S(2)}) async-start(), calls=%async_computation.1 | async-start | bytes 4325376 | tf_op jit(solution)/shard_map/all_gather | solution.py:164
  8.1 20.1 %copy-start.7 = (bf16[4,8,64,64]{3,2,1,0:T(8,128)(2,1)S(1)}, bf16[4,8,64,64]{3,2,1,0:T(8,128)(2,1)}, u32[]{:S(2)}) copy-start(bf16[4,8,64,64]{3,2,1,0:T(8,128)(2,1)} %param.31) | copy-start | bytes 786436
  12.6 19.0 %copy-start.5 = (bf16[4,8,64,64]{3,2,1,0:T(8,128)(2,1)S(1)}, bf16[4,8,64,64]{3,2,1,0:T(8,128)(2,1)}, u32[]{:S(2)}) copy-start(bf16[4,8,64,64]{3,2,1,0:T(8,128)(2,1)} %param.30) | copy-start | bytes 786436
  15.5 18.4 %copy-start.3 = (bf16[512,512]{1,0:T(8,128)(2,1)S(1)}, bf16[512,512]{1,0:T(8,128)(2,1)}, u32[]{:S(2)}) copy-start(bf16[512,512]{1,0:T(8,128)(2,1)} %param.23) | copy-start | bytes 1572868
  15.5 20.9 %copy-start.4 = (bf16[512,512]{1,0:T(8,128)(2,1)S(1)}, bf16[512,512]{1,0:T(8,128)(2,1)}, u32[]{:S(2)}) copy-start(bf16[512,512]{1,0:T(8,128)(2,1)} %param.27) | copy-start | bytes 1572868
  15.5 123.8 %all-to-all-start = ((bf16[32,128,512]{1,2,0:T(8,128)(2,1)}), bf16[32,128,512]{1,2,0:T(8,128)(2,1)}, u32[]{:S(2)}, u32[]{:S(2)}) async-start(bf16[32,128,512]{1,2,0:T(8,128)(2,1)} %stack.2), calls=%async_computation | async-start | bytes 8388608 | tf_op jit(solution)/shard_map/all_to_all | solution.py:166
  25.4 13.8 %copy-start.10 = (f32[4,8]{1,0:T(4,128)S(1)}, f32[4,8]{1,0:T(4,128)}, u32[]{:S(2)}) copy-start(f32[4,8]{1,0:T(4,128)} %param.32) | copy-start | bytes 388
  25.4 15.7 %copy-start.9 = (s32[4,8]{1,0:T(4,128)S(1)}, s32[4,8]{1,0:T(4,128)}, u32[]{:S(2)}) copy-start(s32[4,8]{1,0:T(4,128)} %param.38) | copy-start | bytes 388
  25.4 15.7 %copy-start.14 = (s32[4,8]{1,0:T(4,128)S(1)}, s32[4,8]{1,0:T(4,128)}, u32[]{:S(2)}) copy-start(s32[4,8]{1,0:T(4,128)} %param.37) | copy-start | bytes 388
  25.4 248.7 %all-gather.7.cloned.1.call-start = ((), (), s32[]{:S(2)}) async-start(), calls=%async_computation.2 | async-start | bytes 1179648 | tf_op jit(solution)/shard_map/all_gather | solution.py:175
  33.1 241.0 %all-gather.9.cloned.1.call-start = ((), (), s32[]{:S(2)}) async-start(), calls=%async_computation.3 | async-start | bytes 1179648 | tf_op jit(solution)/shard_map/all_gather | solution.py:174
  41.1 4.7 %copy-start.6 = (s32[4,2,128,128]{3,2,1,0:T(8,128)S(1)}, s32[4,2,128,128]{3,2,1,0:T(8,128)}, u32[]{:S(2)}) copy-start(s32[4,2,128,128]{3,2,1,0:T(8,128)} %param.39) | copy-start | bytes 1572868
  41.1 4.8 %copy-start.11 = (s32[4,2]{0,1:T(2,128)S(1)}, s32[4,2]{0,1:T(2,128)}, u32[]{:S(2)}) copy-start(s32[4,2]{0,1:T(2,128)} %param.40) | copy-start | bytes 100
  41.1 4.9 %copy-start.15 = (s32[4,2]{0,1:T(2,128)S(1)}, s32[4,2]{0,1:T(2,128)}, u32[]{:S(2)}) copy-start(s32[4,2]{0,1:T(2,128)} %param.41) | copy-start | bytes 100
  274.2 33.8 %copy-start.8 = (f32[512]{0:T(512)S(1)}, f32[512]{0:T(512)}, u32[]{:S(2)}) copy-start(f32[512]{0:T(512)} %param.35) | copy-start | bytes 6148
  274.2 1.1 copy-start.1
  277.2 6.7 %copy-start.2 = (f32[512,8,64]{0,2,1:T(8,128)S(1)}, f32[512,8,64]{0,2,1:T(8,128)}, u32[]{:S(2)}) copy-start(f32[512,8,64]{0,2,1:T(8,128)} %copy-done.1) | copy-start | bytes 3145732 | tf_op jit(solution)/shard_map/while
  289.0 1.1 copy-start.1
  292.0 6.7 %copy-start.2 = (f32[512,8,64]{0,2,1:T(8,128)S(1)}, f32[512,8,64]{0,2,1:T(8,128)}, u32[]{:S(2)}) copy-start(f32[512,8,64]{0,2,1:T(8,128)} %copy-done.1) | copy-start | bytes 3145732 | tf_op jit(solution)/shard_map/while
Sparse Core Ops, SparseCore 0:
  10.1 133.3 all-gather.4
  146.1 52.4 all-gather.6
  201.2 50.2 all-gather.8
